TPU v7x, 32 devices: a whole 2x2x4 slice. The times are simulated.
32 devices in a mesh: section: 2 (over x), expert: 16 (over z, y, core).
Axes of the slice: x: 2, y: 2, z: 4, core: 2. Of those that a mesh axis runs over, the one named last changes fastest.
Arguments:
- out_grad: bfloat16 [2, 512, 2048], P('section', 'expert'), may hold values from -6 to 6
- layer_input: bfloat16 [2, 512, 2048], P('section', 'expert'), may hold values from -6 to 6
- router_weight: bfloat16 [2, 2048, 16], P('section'), may hold values from -0.125 to 0.125
- expert_ids: int32 [2, 512, 8], P('section', 'expert'), may hold values from 0 to 15, all different within a row; in each aligned block of 32 rows (0 to 31, 32 to 63, ..., all dimensions but the last counted through in order) at most 24 rows name the same one
- hidden_act: bfloat16 [2, 16, 384, 384], P('section', 'expert'), may hold values from -6 to 6
- down_weight: bfloat16 [2, 16, 384, 2048], P('section', 'expert'), may hold values from -0.3125 to 0.3125
Outputs:
- sent_grad: bfloat16 [2, 512, 2048], P('section', 'expert')
- hidden_grad: bfloat16 [2, 16, 384, 384], P('section', 'expert')
- router_grad: float32 [2, 2048, 16], P('section', 'expert')
Inputs may be any that keep to these rules, and one draw needn't show every extreme that they name: `expert_ids`: each token names 8 different experts. In each aligned block of 32 tokens (the tokens of one device) no expert is named by more than 24 tokens, a bound that some block reaches.
All inputs are finite; a program needn't handle non-finite values.
Results may differ from a plain program's by a relative error of at most 0.0095.
Values may be sent and summed in bfloat16 or wider, within the bound.
A program may use at most 64 MiB of HBM per device.

v0:
```python
import jax
import jax.numpy as jnp
from jax import lax
from jax.sharding import PartitionSpec as P


def shifted(shard, axis, by):
    count = lax.axis_size(axis)
    return lax.ppermute(shard, axis, [(i, (i + by) % count) for i in range(count)])


def shards(out_grad, layer_input, router_weight, expert_ids, hidden_act, down_weight):
    out_grads = out_grad[0]
    inputs = layer_input[0]
    router = router_weight[0]
    chosen_ids = expert_ids[0]
    hidden = hidden_act[0, 0]
    w_down = down_weight[0, 0]
    peer_count = lax.axis_size("expert")
    tokens_here = chosen_ids.shape[0]
    choices_per = chosen_ids.shape[1]
    experts = router.shape[1]
    capacity = hidden.shape[0] // peer_count
    logits = jnp.dot(inputs, router, preferred_element_type=jnp.float32)
    picked = (chosen_ids[:, :, None] == jnp.arange(experts, dtype=jnp.int32)[None, None, :]).astype(
        jnp.float32
    )
    chosen_logits = jnp.sum(picked * logits[:, None, :], axis=-1)
    weights = jnp.exp(chosen_logits)
    gate_vals = (weights / jnp.sum(weights, axis=-1, keepdims=True)).astype(jnp.bfloat16)
    flat_hot = picked.reshape(tokens_here * choices_per, experts)
    before = jnp.cumsum(flat_hot, axis=0) - flat_hot
    slot_rank = (
        jnp.sum(before * flat_hot, axis=-1).astype(jnp.int32).reshape(tokens_here, choices_per)
    )
    position = chosen_ids * capacity + slot_rank
    placing = (
        position[:, :, None] == jnp.arange(experts * capacity, dtype=jnp.int32)[None, None, :]
    ).astype(jnp.bfloat16)
    send_grads = jnp.einsum(
        "tks,td->sd", placing, out_grads, preferred_element_type=jnp.float32
    ).astype(jnp.bfloat16)
    send_gates = jnp.einsum(
        "tks,tk->s", placing, gate_vals, preferred_element_type=jnp.float32
    ).astype(jnp.bfloat16)
    send_grads = send_grads.reshape(experts, capacity, send_grads.shape[-1])
    send_gates = send_gates.reshape(experts, capacity)
    recv_grads, recv_gates = (
        lax.all_to_all(send_grads, "expert", split_axis=0, concat_axis=0, tiled=True),
        lax.all_to_all(send_gates, "expert", split_axis=0, concat_axis=0, tiled=True),
    )
    slot_rows = recv_grads.reshape(-1, recv_grads.shape[-1])
    expert_out = jnp.dot(hidden, w_down, preferred_element_type=jnp.float32)
    slot_dg = jnp.sum(slot_rows.astype(jnp.float32) * expert_out, axis=-1)
    scaled = (
        recv_gates.reshape(-1).astype(jnp.float32)[:, None] * slot_rows.astype(jnp.float32)
    ).astype(jnp.bfloat16)
    hidden_grad = lax.dot_general(
        scaled, w_down, (((1,), (1,)), ((), ())), preferred_element_type=jnp.float32
    ).astype(jnp.bfloat16)
    returned = lax.all_to_all(
        slot_dg.reshape(peer_count, capacity), "expert", split_axis=0, concat_axis=0, tiled=True
    )
    gate_grad = jnp.take(returned.reshape(-1), position, axis=0)
    gate_float = gate_vals.astype(jnp.float32)
    dchosen = gate_float * (gate_grad - jnp.sum(gate_float * gate_grad, axis=-1, keepdims=True))
    logit_grad = jnp.sum(dchosen[:, :, None] * picked, axis=1).astype(jnp.bfloat16)
    router_part = lax.dot_general(
        logit_grad, router, (((1,), (1,)), ((), ())), preferred_element_type=jnp.float32
    )
    input_grad = (out_grads.astype(jnp.float32) + router_part).astype(jnp.bfloat16)
    to_previous = shifted(input_grad[None], "section", -1)
    router_grad = lax.psum_scatter(
        jnp.einsum("td,te->de", inputs, logit_grad, preferred_element_type=jnp.float32),
        "expert",
        scatter_dimension=0,
        tiled=True,
    )
    return (to_previous, hidden_grad[None, None], router_grad[None])


def solution(mesh):
    placed = (
        P("section", "expert", None),
        P("section", "expert", None),
        P("section", None, None),
        P("section", "expert", None),
        P("section", "expert", None, None),
        P("section", "expert", None, None),
    )
    return jax.shard_map(
        shards,
        mesh=mesh,
        in_specs=placed,
        out_specs=(
            P("section", "expert", None),
            P("section", "expert", None, None),
            P("section", "expert", None),
        ),
        check_vma=False,
    )
```

profile of v0, /device:TPU:0, one launch (start us, length us, event | category | flops | bytes accessed | tf_op | source)
XLA Modules:
  0.0 144.4 jit_solution(12251235587889434299)
XLA Ops:
  7.2 0.9 copy.32
  8.1 0.1 eq.55
  8.1 0.1 eq.51
  8.3 0.6 reduce-window.6
  8.8 0.2 slice_reduce_fusion
  9.0 0.1 fusion.23
  9.3 0.7 multiply_add_fusion
  10.1 0.2 convert_reduce_fusion
  10.3 2.6 %convolution_convert_fusion = bf16[384,2048]{1,0:T(8,128)(2,1)} fusion(bf16[32,384]{1,0:T(8,128)(2,1)S(1)} %convert_reduce_fusion, bf16[1,32,2048]{2,1,0:T(8,128)(2,1)} %param.6), kind=kOutput, calls=%fused_computation.4 | convolution fusion | flops 50331648 | bytes 1728512 | tf_op jit(solution)/shard_map/tks,td->sd/dot_general | solution.py:40
  12.9 7.5 %all-to-all-start = ((bf16[16,24,2048]{2,1,0:T(8,128)(2,1)}), bf16[16,24,2048]{2,1,0:T(8,128)(2,1)S(1)}, u32[]{:S(2)}, u32[]{:S(2)}) async-start(bf16[16,24,2048]{2,1,0:T(8,128)(2,1)} %bitcast.73), calls=%async_computation | async-start | bytes 3145728 | tf_op jit(solution)/shard_map/all_to_all | solution.py:49
  20.6 0.1 reshape.167
  20.7 0.1 fusion.16
  20.9 31.6 %all-to-all-done = bf16[16,24,2048]{2,1,0:T(8,128)(2,1)S(1)} async-done(((bf16[16,24,2048]{2,1,0:T(8,128)(2,1)}), bf16[16,24,2048]{2,1,0:T(8,128)(2,1)S(1)}, u32[]{:S(2)}, u32[]{:S(2)}) %all-to-all-start) | async-done | bytes 1572896 | tf_op jit(solution)/shard_map/all_to_all | solution.py:49
  52.4 2.0 %fusion = f32[384]{0:T(512)S(1)} fusion(bf16[1,1,384,2048]{3,2,1,0:T(8,128)(2,1)S(1)} %copy-done, bf16[16,24,2048]{2,1,0:T(8,128)(2,1)S(1)} %all-to-all-done, bf16[1,1,384,384]{3,2,1,0:T(8,128)(2,1)} %param.10), kind=kOutput, calls=%fused_computation.2 | convolution fusion | flops 606338688 | bytes 3442176 | tf_op jit(solution)/shard_map/dot_general | solution.py:53
  54.5 0.7 all_to_all.16
  55.2 9.1 %all-to-all-start.1 = ((f32[16,1,24]{2,1,0:T(1,128)}), f32[16,1,24]{2,1,0:T(1,128)S(1)}, u32[]{:S(2)}, u32[]{:S(2)}) async-start(f32[16,1,24]{2,1,0:T(1,128)} %all_to_all.16), calls=%async_computation.1 | async-start | bytes 16384 | tf_op jit(solution)/shard_map/all_to_all | solution.py:61
  64.3 6.3 %all-to-all-done.1 = f32[16,1,24]{2,1,0:T(1,128)S(1)} async-done(((f32[16,1,24]{2,1,0:T(1,128)}), f32[16,1,24]{2,1,0:T(1,128)S(1)}, u32[]{:S(2)}, u32[]{:S(2)}) %all-to-all-start.1) | async-done | bytes 1568 | tf_op jit(solution)/shard_map/all_to_all | solution.py:61
  70.6 0.5 broadcast.118
  71.1 0.7 reduce.7
  71.9 1.9 %gather_fusion = f32[256]{0:T(256)S(1)} fusion(f32[384]{0:T(512)S(1)} %reshape.162, s32[1024]{0:T(1024)S(1)} %pad_clamp_fusion), kind=kCustom, calls=%fused_computation | custom fusion | bytes 3072 | tf_op jit(solution)/shard_map/jit(_take)/gather | solution.py:64
  74.1 0.1 copy.40
  74.2 0.3 convolution_reduce_fusion
  74.4 0.7 all_to_all.20
  75.1 3.5 %all-to-all-start.2 = ((bf16[16,1,24]{2,1,0:T(2,128)(2,1)}), bf16[16,1,24]{2,1,0:T(2,128)(2,1)S(1)}, u32[]{:S(2)}, u32[]{:S(2)}) async-start(bf16[16,1,24]{2,1,0:T(2,128)(2,1)} %all_to_all.20), calls=%async_computation.2 | async-start | bytes 16384 | tf_op jit(solution)/shard_map/all_to_all | solution.py:50
  78.7 0.8 convolution_bitcast_fusion
  79.5 0.9 fusion.2
  80.4 1.6 %collective-permute-start = (bf16[1,32,2048]{2,1,0:T(8,128)(2,1)}, bf16[1,32,2048]{2,1,0:T(8,128)(2,1)S(1)}, u32[]{:S(2)}, u32[]{:S(2)}) collective-permute-start(bf16[1,32,2048]{2,1,0:T(8,128)(2,1)} %fusion.2), channel_id=1, source_target_pairs={{0,16},{16,0},{1,17},{17,1},{2,18},{18,2},{3,19},{19,3},{4,20},{20... | collective-permute-start | bytes 393224 | tf_op jit(solution)/shard_map/ppermute | solution.py:9
  81.9 3.0 %all-to-all-done.2 = bf16[16,1,24]{2,1,0:T(2,128)(2,1)S(1)} async-done(((bf16[16,1,24]{2,1,0:T(2,128)(2,1)}), bf16[16,1,24]{2,1,0:T(2,128)(2,1)S(1)}, u32[]{:S(2)}, u32[]{:S(2)}) %all-to-all-start.2) | async-done | bytes 800 | tf_op jit(solution)/shard_map/all_to_all | solution.py:50
  84.9 0.3 multiply_convert_fusion
  85.3 1.7 %fusion.9 = bf16[1,1,384,384]{3,2,1,0:T(8,128)(2,1)} fusion(bf16[384,2048]{1,0:T(8,128)(2,1)S(1)} %bitcast.74, bf16[1,1,384,2048]{3,2,1,0:T(8,128)(2,1)S(1)} %copy-done), kind=kOutput, calls=%fused_computation.13 | convolution fusion | flops 604127232 | bytes 3440640 | tf_op jit(solution)/shard_map/dot_general | solution.py:58
  87.0 49.9 %reduce-scatter.2.cloned.1.call-done = f32[128,16]{0,1:T(8,128)} async-done(((f32[2048,16]{0,1:T(8,128)}), f32[128,16]{0,1:T(8,128)}) %reduce-scatter.2.cloned.1.call-update) | async-done | bytes 8208 | tf_op jit(solution)/shard_map/reduce_scatter | solution.py:73
  136.9 0.7 copy.44
  (32 shorter events, 0.8 us)
Async XLA Ops:
  7.2 45.3 %copy-start = (bf16[1,1,384,2048]{3,2,1,0:T(8,128)(2,1)S(1)}, bf16[1,1,384,2048]{3,2,1,0:T(8,128)(2,1)}, u32[]{:S(2)}) copy-start(bf16[1,1,384,2048]{3,2,1,0:T(8,128)(2,1)} %param.11) | copy-start | bytes 4718596
  12.9 7.7 %copy-start.1 = (bf16[1,32,2048]{2,1,0:T(8,128)(2,1)S(1)}, bf16[1,32,2048]{2,1,0:T(8,128)(2,1)}, u32[]{:S(2)}) copy-start(bf16[1,32,2048]{2,1,0:T(8,128)(2,1)} %param.7) | copy-start | bytes 393220
  12.9 7.7 %copy-start.3 = (bf16[1,2048,16]{1,2,0:T(8,128)(2,1)S(1)}, bf16[1,2048,16]{1,2,0:T(8,128)(2,1)}, u32[]{:S(2)}) copy-start(bf16[1,2048,16]{1,2,0:T(8,128)(2,1)} %param.8) | copy-start | bytes 196612
  12.9 7.9 %copy-start.4 = (s32[1,32,8]{1,2,0:T(8,128)S(1)}, s32[1,32,8]{1,2,0:T(8,128)}, u32[]{:S(2)}) copy-start(s32[1,32,8]{1,2,0:T(8,128)} %param.9) | copy-start | bytes 3076
  12.9 39.5 %all-to-all-start = ((bf16[16,24,2048]{2,1,0:T(8,128)(2,1)}), bf16[16,24,2048]{2,1,0:T(8,128)(2,1)S(1)}, u32[]{:S(2)}, u32[]{:S(2)}) async-start(bf16[16,24,2048]{2,1,0:T(8,128)(2,1)} %bitcast.73), calls=%async_computation | async-start | bytes 3145728 | tf_op jit(solution)/shard_map/all_to_all | solution.py:49
  55.2 15.4 %all-to-all-start.1 = ((f32[16,1,24]{2,1,0:T(1,128)}), f32[16,1,24]{2,1,0:T(1,128)S(1)}, u32[]{:S(2)}, u32[]{:S(2)}) async-start(f32[16,1,24]{2,1,0:T(1,128)} %all_to_all.16), calls=%async_computation.1 | async-start | bytes 16384 | tf_op jit(solution)/shard_map/all_to_all | solution.py:61
  71.9 7.6 %copy-start.2 = (bf16[1,32,2048]{2,1,0:T(8,128)(2,1)S(1)}, bf16[1,32,2048]{2,1,0:T(8,128)(2,1)}, u32[]{:S(2)}) copy-start(bf16[1,32,2048]{2,1,0:T(8,128)(2,1)} %param.6) | copy-start | bytes 393220
  75.1 9.8 %all-to-all-start.2 = ((bf16[16,1,24]{2,1,0:T(2,128)(2,1)}), bf16[16,1,24]{2,1,0:T(2,128)(2,1)S(1)}, u32[]{:S(2)}, u32[]{:S(2)}) async-start(bf16[16,1,24]{2,1,0:T(2,128)(2,1)} %all_to_all.20), calls=%async_computation.2 | async-start | bytes 16384 | tf_op jit(solution)/shard_map/all_to_all | solution.py:50
  78.6 58.3 %reduce-scatter.2.cloned.1.call-start = ((), (), s32[]{:S(2)}) async-start(), calls=%async_computation.4 | async-start | bytes 139264 | tf_op jit(solution)/shard_map/reduce_scatter | solution.py:73
  80.4 6.6 %collective-permute-start = (bf16[1,32,2048]{2,1,0:T(8,128)(2,1)}, bf16[1,32,2048]{2,1,0:T(8,128)(2,1)S(1)}, u32[]{:S(2)}, u32[]{:S(2)}) collective-permute-start(bf16[1,32,2048]{2,1,0:T(8,128)(2,1)} %fusion.2), channel_id=1, source_target_pairs={{0,16},{16,0},{1,17},{17,1},{2,18},{18,2},{3,19},{19,3},{4,20},{20... | collective-permute-start | bytes 393224 | tf_op jit(solution)/shard_map/ppermute | solution.py:9
Sparse Core Ops, SparseCore 0:
  83.4 53.4 reduce-scatter.1
where the time goes:
time: 145 us; the launch traced here: 144 us
  waiting for transfers between devices  90.8 us (63%)
  starting transfers between devices  21.7 us (15%)
  between operations  14.2 us (10%)
  matrix products  8.45 us (6%)
  local copies, waits for them, and re-layouts  6.49 us (4%)
  other arithmetic  2.76 us (2%)
    reduce_scatter x1, waiting for transfers between devices, shards(): lax.psum_scatter(jnp.einsum('td,te->de', inputs, logit_grad, preferred_el...  49.9 us
    all_to_all x1, waiting for transfers between devices, shards(): lax.all_to_all(send_grads, 'expert', split_axis=0, concat_axis=0, tiled=T...  31.6 us
    all_to_all x1, starting transfers between devices, shards(): lax.all_to_all(slot_dg.reshape(peer_count, capacity), 'expert', split_axi...  9.11 us
    all_to_all x1, starting transfers between devices, shards(): lax.all_to_all(send_grads, 'expert', split_axis=0, concat_axis=0, tiled=T...  7.52 us
    all_to_all x1, waiting for transfers between devices, shards(): lax.all_to_all(slot_dg.reshape(peer_count, capacity), 'expert', split_axi...  6.32 us
    all_to_all x1, starting transfers between devices, shards(): lax.all_to_all(send_gates, 'expert', split_axis=0, concat_axis=0, tiled=T...  3.47 us
    all_to_all x1, waiting for transfers between devices, shards(): lax.all_to_all(send_gates, 'expert', split_axis=0, concat_axis=0, tiled=T...  3.01 us
  transfers between devices with their start and end apart: 5, of which 4 were waited for; matrix products, arithmetic and copies ran while one was open for 3% of the time, Pallas kernels for 0%

commit v1 on v0

v1 whole, which is shorter than its diff:
```python
import functools

import jax
import jax.numpy as jnp
from jax import lax
from jax.experimental import pallas as pl
from jax.experimental.pallas import tpu as pltpu
from jax.sharding import PartitionSpec as P

MESH = pl.DeviceIdType.MESH
NT = (((1,), (1,)), ((), ()))
TN = (((0,), (0,)), ((), ()))
NN = (((1,), (0,)), ((), ()))
LANES = 128
ROWS_A = 4
CHUNKS = 2
A_UP, A_DOWN, B_NEXT, B_PREV, SIB = range(5)


def dot(lhs, rhs, dims):
    return lax.dot_general(lhs, rhs, dims, preferred_element_type=jnp.float32)


def kernel(
    sections, n, og, x, rt, ids, hid, w, out_g, out_h, out_r,
    xg, xs, meta, dgb, ogn, rtn, lgn, xv, rtv, idv, hv, wv,
    gt, sel, hs, u, v, dgo, dg2, lg, outv, hgv, rgv,
    blk_recv, blk_send, meta_recv, meta_send, slab_recv, slab_send,
    dg_recv, dg_send, sec_recv, sec_send, loc,
):
    tokens, d_model = og.shape
    topk = ids.shape[0]
    experts = rt.shape[0]
    slots, f_dim = hid.shape
    cap = slots // n
    feats = out_r.shape[1]
    per_tile = LANES // tokens
    tiles = n // per_tile
    nb = n // (2 * ROWS_A)
    tiles_per_group = tiles // ROWS_A
    rows = tokens // CHUNKS

    me = lax.axis_index("expert")
    sec = lax.axis_index("section")
    c = lax.rem(me, 2)
    b = lax.rem(me // 2, nb)
    a = me // (2 * nb)
    sib = me + 1 - 2 * c
    prev = lax.rem(sec + sections - 1, sections)
    nxt = lax.rem(sec + 1, sections)
    tile = me // per_tile
    offset = lax.rem(me, per_tile) * tokens

    local = [
        pltpu.make_async_copy(x, xv, loc.at[0]),
        pltpu.make_async_copy(rt, rtv, loc.at[1]),
        pltpu.make_async_copy(ids, idv, loc.at[2]),
        pltpu.make_async_copy(og, xg.at[me], loc.at[3]),
        pltpu.make_async_copy(w, wv, loc.at[4]),
        pltpu.make_async_copy(hid, hv, loc.at[5]),
    ]
    for copy in local:
        copy.start()

    barrier = pltpu.get_barrier_semaphore()

    def greet(d, carry):
        pl.semaphore_signal(
            barrier, inc=1, device_id={"expert": lax.rem(me + d, n)}, device_id_type=MESH
        )
        return carry

    lax.fori_loop(1, n, greet, 0)
    near = (prev,) if sections == 2 else (prev, nxt)
    for other in near:
        pl.semaphore_signal(barrier, inc=1, device_id={"section": other}, device_id_type=MESH)
    pl.semaphore_wait(barrier, n - 1 + len(near))

    def block_copy(idx, q, target, way, own=False):
        part = pl.ds(q * rows, rows)
        return pltpu.make_async_remote_copy(
            src_ref=og.at[part] if own else xg.at[idx, part],
            dst_ref=xg.at[idx, part],
            send_sem=blk_send.at[idx, q, way],
            recv_sem=blk_recv.at[idx, q],
            device_id={"expert": target},
            device_id_type=MESH,
        )

    def column_sends(g, q, do, own=False):
        idx = (g * nb + b) * 2 + c

        @pl.when(jnp.logical_and(g <= a, a < ROWS_A - 1))
        def _():
            do(block_copy(idx, q, me + 2 * nb, A_UP, own))

        @pl.when(jnp.logical_and(g >= a, a > 0))
        def _():
            do(block_copy(idx, q, me - 2 * nb, A_DOWN, own))

        @pl.when(b < nb - 1)
        def _():
            do(block_copy(idx, q, me + 2, B_NEXT, own))

        @pl.when(b > 0)
        def _():
            do(block_copy(idx, q, me - 2, B_PREV, own))

        do(block_copy(idx, q, sib, SIB, own))

    def cross_sends(g, b2, q, do):
        idx = (g * nb + b2) * 2 + c
        if nb > 2:
            @pl.when(jnp.logical_and(b2 < b, b < nb - 1))
            def _():
                do(block_copy(idx, q, me + 2, B_NEXT))

            @pl.when(jnp.logical_and(b2 > b, b > 0))
            def _():
                do(block_copy(idx, q, me - 2, B_PREV))

        do(block_copy(idx, q, sib, SIB))

    def section_copy(i, src, dst):
        return pltpu.make_async_remote_copy(
            src_ref=src, dst_ref=dst, send_sem=sec_send.at[i], recv_sem=sec_recv.at[i],
            device_id={"section": prev}, device_id_type=MESH,
        )

    grads_over = section_copy(0, og, ogn)
    router_over = section_copy(1, rt, rtn)
    logit_over = section_copy(2, lg.at[tile], lgn)

    def slab_copy(peer):
        lane = pl.multiple_of((peer * feats) // LANES * LANES, LANES)
        return pltpu.make_async_remote_copy(
            src_ref=x.at[:, pl.ds(lane, LANES)], dst_ref=xs.at[me],
            send_sem=slab_send.at[peer], recv_sem=slab_recv.at[me],
            device_id={"expert": peer}, device_id_type=MESH,
        )

    def meta_copy(peer):
        return pltpu.make_async_remote_copy(
            src_ref=meta.at[me], dst_ref=meta.at[me],
            send_sem=meta_send.at[peer], recv_sem=meta_recv.at[me],
            device_id={"expert": peer}, device_id_type=MESH,
        )

    def dg_copy(peer):
        return pltpu.make_async_remote_copy(
            src_ref=dgo, dst_ref=dgb.at[me],
            send_sem=dg_send.at[peer], recv_sem=dg_recv.at[me],
            device_id={"expert": peer}, device_id_type=MESH,
        )

    def await_from(peer, dst, sem):
        pltpu.make_async_remote_copy(
            src_ref=dst, dst_ref=dst, send_sem=sem, recv_sem=sem,
            device_id={"expert": peer}, device_id_type=MESH,
        ).wait_recv()

    def each_peer(fn):
        def step(d, carry):
            fn(lax.rem(me + d, n))
            return carry

        lax.fori_loop(1, n, step, 0)

    start = lambda copy: copy.start()
    finish = lambda copy: copy.wait_send()

    for q in range(CHUNKS):
        column_sends(a, q, start, own=True)
    grads_over.start()
    router_over.start()

    own_lane = pl.multiple_of((me * feats) // LANES * LANES, LANES)
    own_slab = pltpu.make_async_copy(x.at[:, pl.ds(own_lane, LANES)], xs.at[me], loc.at[6])
    own_slab.start()
    for copy in local[:3]:
        copy.wait()
    logits = dot(rtv[...], xv[...], NT)
    row = lax.broadcasted_iota(jnp.int32, (experts, tokens), 0)
    named = row == idv[0:1, :]
    for k in range(1, topk):
        named = jnp.logical_or(named, row == idv[k : k + 1, :])
    weights = jnp.where(named, jnp.exp(logits), 0.0)
    gates = weights / jnp.sum(weights, axis=0, keepdims=True)
    marked = jnp.where(named, gates, -1.0).astype(jnp.bfloat16)
    token_of = lax.broadcasted_iota(jnp.int32, (tokens, LANES), 0)
    lane_of = lax.broadcasted_iota(jnp.int32, (tokens, LANES), 1)
    place = jnp.where(lane_of == token_of + offset, 1.0, 0.0).astype(jnp.bfloat16)
    meta[me] = dot(marked, place, NN).astype(jnp.bfloat16)
    each_peer(lambda peer: meta_copy(peer).start())
    each_peer(lambda peer: slab_copy(peer).start())
    for copy in local[3:]:
        copy.wait()

    def order(k):
        closest = jnp.minimum(a, ROWS_A - 1 - a)
        d = (k + 1) // 2
        both = jnp.where(lax.rem(k, 2) == 1, a - d, a + d)
        rest = jnp.where(a <= ROWS_A - 1 - a, k, ROWS_A - 1 - k)
        return jnp.where(k <= 2 * closest, both, rest)

    def slots_of_expert():
        each_peer(lambda peer: await_from(peer, meta.at[peer], meta_recv.at[peer]))
        erow = lax.broadcasted_iota(jnp.int32, (experts, LANES), 0)
        t_from = lax.broadcasted_iota(jnp.int32, (LANES, LANES), 0)
        t_to = lax.broadcasted_iota(jnp.int32, (LANES, LANES), 1)
        ahead = jnp.where(
            jnp.logical_and(t_from < t_to, t_from // tokens == t_to // tokens), 1.0, 0.0
        ).astype(jnp.bfloat16)
        lane_block = lax.broadcasted_iota(jnp.int32, (1, LANES), 1) // tokens
        slot_row = lax.broadcasted_iota(jnp.int32, (slots, LANES), 0)
        for j in range(tiles):
            total = meta[j * per_tile].astype(jnp.float32)
            for i in range(1, per_tile):
                total = total + meta[j * per_tile + i].astype(jnp.float32)
            gt[j] = total
            mine = jnp.sum(jnp.where(erow == me, total, 0.0), axis=0, keepdims=True)
            taken = jnp.where(mine >= 0.0, 1.0, 0.0)
            many = jnp.broadcast_to(taken, (16, LANES)).astype(jnp.bfloat16)
            rank = dot(many, ahead, NN)[0:1, :].astype(jnp.int32)
            slot = (lane_block + j * per_tile) * cap + rank
            slot = jnp.where(mine >= 0.0, slot, -1)
            hot = jnp.where(slot_row == slot, 1.0, 0.0).astype(jnp.bfloat16)
            sel[:, j * LANES : (j + 1) * LANES] = hot
            hs[j] = dot(hv[...], hot, TN)

    def step(k, carry):
        @pl.when(k < ROWS_A - 1)
        def _():
            g = order(k + 1)
            idx = (g * nb + b) * 2 + c
            for q in range(CHUNKS):
                block_copy(idx, q, sib, SIB).wait_recv()
                column_sends(g, q, start)

        g = order(k)
        for j in range(1, nb):
            b2 = lax.rem(b + j, nb)
            idx = (g * nb + b2) * 2 + c
            for q in range(CHUNKS):
                block_copy(idx, q, sib, SIB).wait_recv()
                cross_sends(g, b2, q, start)
        for b2 in range(nb):
            idx = (g * nb + b2) * 2 + 1 - c
            for q in range(CHUNKS):
                block_copy(idx, q, sib, SIB).wait_recv()

        @pl.when(k == ROWS_A - 2)
        def _():
            slots_of_expert()

        for i in range(tiles_per_group):
            t = g * tiles_per_group + i
            u[t] = dot(
                wv[...], xg[pl.ds(t * per_tile, per_tile)].reshape(LANES, d_model), NT
            )
        return carry

    lax.fori_loop(0, ROWS_A, step, 0)

    for j in range(tiles):
        dgo[j : j + 1, :] = jnp.sum(u[j] * hs[j], axis=0, keepdims=True)
    each_peer(lambda peer: dg_copy(peer).start())

    erow = lax.broadcasted_iota(jnp.int32, (experts, LANES), 0)
    for j in range(tiles):
        mine = jnp.sum(jnp.where(erow == me, gt[j], 0.0), axis=0, keepdims=True)
        v[:, j * LANES : (j + 1) * LANES] = (u[j] * jnp.maximum(mine, 0.0)).astype(jnp.bfloat16)
    hgv[...] = dot(sel[...], v[...], NT).astype(jnp.bfloat16)
    hidden_out = pltpu.make_async_copy(hgv, out_h, loc.at[7])
    hidden_out.start()

    own_slab.wait()
    each_peer(lambda peer: await_from(peer, xs.at[peer], slab_recv.at[peer]))
    grads_over.wait_recv()
    router_over.wait_recv()

    for j in range(tiles):
        dg2[j, pl.ds(me, 1), :] = dgo[j : j + 1, :]

    def take(peer):
        await_from(peer, dgb.at[peer], dg_recv.at[peer])
        for j in range(tiles):
            dg2[j, pl.ds(peer, 1), :] = dgb[peer, j : j + 1, :]

    each_peer(take)
    for j in range(tiles):
        g = jnp.maximum(gt[j], 0.0)
        d = dg2[j]
        lg[j] = (g * (d - jnp.sum(g * d, axis=0, keepdims=True))).astype(jnp.bfloat16)
    logit_over.start()

    lg_all = jnp.concatenate([lg[j] for j in range(tiles)], axis=1)
    part = dot(lg_all, xs[...].reshape(n * tokens, LANES), NN)
    if feats < LANES:
        shift = lax.rem(LANES - lax.rem(me * feats, LANES), LANES)
        part = pltpu.roll(part, shift, 1)[:, :feats]
    rgv[...] = part
    router_out = pltpu.make_async_copy(rgv, out_r, loc.at[8])
    router_out.start()

    logit_over.wait_recv()
    mine = dot(place, lgn[...], NT).astype(jnp.bfloat16)
    outv[...] = (ogn[...].astype(jnp.float32) + dot(mine, rtn[...], NN)).astype(jnp.bfloat16)
    grads_out = pltpu.make_async_copy(outv, out_g, loc.at[9])
    grads_out.start()

    for q in range(CHUNKS):
        column_sends(a, q, finish, own=True)

    def drain(k, carry):
        g = order(k)

        @pl.when(k > 0)
        def _():
            for q in range(CHUNKS):
                column_sends(g, q, finish)

        for j in range(1, nb):
            for q in range(CHUNKS):
                cross_sends(g, lax.rem(b + j, nb), q, finish)
        return carry

    lax.fori_loop(0, ROWS_A, drain, 0)

    def sent(peer):
        meta_copy(peer).wait_send()
        slab_copy(peer).wait_send()
        dg_copy(peer).wait_send()

    each_peer(sent)
    grads_over.wait_send()
    router_over.wait_send()
    logit_over.wait_send()
    hidden_out.wait()
    router_out.wait()
    grads_out.wait()


def shards(sections, n, out_grad, layer_input, router_weight, expert_ids, hidden_act, down_weight):
    og, x, hid, w = out_grad[0], layer_input[0], hidden_act[0, 0], down_weight[0, 0]
    rt, ids = router_weight[0].T, expert_ids[0].T
    tokens, d_model = og.shape
    experts, topk = rt.shape[0], ids.shape[0]
    slots, f_dim = hid.shape
    feats = d_model // n
    total = n * tokens
    tiles = total // LANES
    bf16, f32 = jnp.bfloat16, jnp.float32
    dma = pltpu.SemaphoreType.DMA
    hbm = pl.BlockSpec(memory_space=pl.ANY)
    grads, hidden, router = pl.pallas_call(
        functools.partial(kernel, sections, n),
        out_shape=(
            jax.ShapeDtypeStruct((tokens, d_model), bf16),
            jax.ShapeDtypeStruct((slots, f_dim), bf16),
            jax.ShapeDtypeStruct((experts, feats), f32),
        ),
        in_specs=[hbm] * 6,
        out_specs=(hbm,) * 3,
        scratch_shapes=[
            pltpu.VMEM((n, tokens, d_model), bf16),
            pltpu.VMEM((n, tokens, LANES), bf16),
            pltpu.VMEM((n, experts, LANES), bf16),
            pltpu.VMEM((n, tiles, LANES), f32),
            pltpu.VMEM((tokens, d_model), bf16),
            pltpu.VMEM((experts, d_model), bf16),
            pltpu.VMEM((experts, LANES), bf16),
            pltpu.VMEM((tokens, d_model), bf16),
            pltpu.VMEM((experts, d_model), bf16),
            pltpu.VMEM((topk, tokens), jnp.int32),
            pltpu.VMEM((slots, f_dim), bf16),
            pltpu.VMEM((f_dim, d_model), bf16),
            pltpu.VMEM((tiles, experts, LANES), f32),
            pltpu.VMEM((slots, total), bf16),
            pltpu.VMEM((tiles, f_dim, LANES), f32),
            pltpu.VMEM((tiles, f_dim, LANES), f32),
            pltpu.VMEM((f_dim, total), bf16),
            pltpu.VMEM((tiles, LANES), f32),
            pltpu.VMEM((tiles, experts, LANES), f32),
            pltpu.VMEM((tiles, experts, LANES), bf16),
            pltpu.VMEM((tokens, d_model), bf16),
            pltpu.VMEM((slots, f_dim), bf16),
            pltpu.VMEM((experts, feats), f32),
            dma((n, CHUNKS)),
            dma((n, CHUNKS, 5)),
            dma((n,)),
            dma((n,)),
            dma((n,)),
            dma((n,)),
            dma((n,)),
            dma((n,)),
            dma((3,)),
            dma((3,)),
            dma((10,)),
        ],
        compiler_params=pltpu.CompilerParams(
            collective_id=0, has_side_effects=True, vmem_limit_bytes=48 * 2**20
        ),
        cost_estimate=pl.CostEstimate(
            flops=2 * total * d_model * f_dim, bytes_accessed=4 * f_dim * d_model, transcendentals=0
        ),
    )(og, x, rt, ids, hid, w)
    return (grads[None], hidden[None, None], router.T[None])


def solution(mesh):
    placed = (
        P("section", "expert", None),
        P("section", "expert", None),
        P("section", None, None),
        P("section", "expert", None),
        P("section", "expert", None, None),
        P("section", "expert", None, None),
    )
    return jax.shard_map(
        functools.partial(shards, mesh.shape["section"], mesh.shape["expert"]),
        mesh=mesh,
        in_specs=placed,
        out_specs=(
            P("section", "expert", None),
            P("section", "expert", None, None),
            P("section", "expert", None),
        ),
        check_vma=False,
    )
```

time: 145 us -> 45.9 us (0.32)
  waiting for transfers between devices: 90.8 us -> 0 us
  Pallas kernels: 0 us -> 37.3 us
  starting transfers between devices: 21.7 us -> 0 us
  between operations: 14.2 us -> 0.65 us
  matrix products: 8.45 us -> 0 us
  other arithmetic: 2.76 us -> 0 us
    reduce_scatter x1 -> x0, waiting for transfers between devices: 49.9 us -> none  [shards(): lax.psum_scatter(jnp.einsum('td,te->de', inputs, logit_grad, preferred_el...]
    all_to_all x3 -> x0, waiting for transfers between devices: 40.9 us -> none  [the longest x1 31.6 us: shards(): lax.all_to_all(send_grads, 'expert', split_axis=0, concat_axis=0, tiled=T...]
    pallas_call x0 -> x1, Pallas kernels: none -> 37.3 us  [shards(): pl.pallas_call(functools.partial(kernel, sections, n), out_shape=(jax.Sha...]
    all_to_all x3 -> x0, starting transfers between devices: 20.1 us -> none  [the longest x1 9.11 us: shards(): lax.all_to_all(slot_dg.reshape(peer_count, capacity), 'expert', split_axi...]
    dot_general x7 -> x0, matrix products: 8.45 us -> none  [the longest x1 2.65 us: shards(): jnp.einsum('tks,td->sd', placing, out_grads, preferred_element_type=jnp.f...]
    unnamed x12 -> x15, local copies, waits for them, and re-layouts: 1.56 us -> 7.66 us
    gather x3 -> x0, local copies, waits for them, and re-layouts: 2.09 us -> none  [shards(): gate_grad = jnp.take(returned.reshape(-1), position, axis=0)]
    all_to_all x3 -> x0, local copies, waits for them, and re-layouts: 1.92 us -> none  [the longest x2 1.22 us: shards(): lax.all_to_all(slot_dg.reshape(peer_count, capacity), 'expert', split_axi...]
  transfers between devices with their start and end apart: 5 -> 0, of which waited for: 4 -> 0; matrix products, arithmetic and copies ran while one was open for 3% -> 0% of each run, Pallas kernels for 0% -> 0%
where the time goes in v1:
time: 45.9 us; the launch traced here: 45.6 us
  Pallas kernels  37.3 us (81%)
  local copies, waits for them, and re-layouts  7.66 us (17%)
  between operations  0.65 us (1%)
    pallas_call x1, Pallas kernels, shards(): pl.pallas_call(functools.partial(kernel, sections, n), out_shape=(jax.Sha...  37.3 us
    unnamed x15, local copies, waits for them, and re-layouts  7.66 us

profile of v1, /device:TPU:0, one launch (start us, length us, event | category | flops | bytes accessed | tf_op | source)
XLA Modules:
  0.0 45.6 jit_solution(2811289945200652016)
XLA Ops:
  0.6 0.0 copy-start
  0.6 1.4 %copy-done = bf16[1,1,384,2048]{3,2,1,0:T(8,128)(2,1)S(1)} copy-done((bf16[1,1,384,2048]{3,2,1,0:T(8,128)(2,1)S(1)}, bf16[1,1,384,2048]{3,2,1,0:T(8,128)(2,1)}, u32[]{:S(2)}) %copy-start) | copy-done | bytes 1572888
  2.0 0.0 copy-start.1
  2.0 1.0 %copy-done.1 = bf16[1,1,384,384]{3,2,1,0:T(8,128)(2,1)S(1)} copy-done((bf16[1,1,384,384]{3,2,1,0:T(8,128)(2,1)S(1)}, bf16[1,1,384,384]{3,2,1,0:T(8,128)(2,1)}, u32[]{:S(2)}) %copy-start.1) | copy-done | bytes 294936
  3.0 0.0 copy-start.2
  3.0 0.9 %copy-done.2 = bf16[1,32,2048]{2,1,0:T(8,128)(2,1)S(1)} copy-done((bf16[1,32,2048]{2,1,0:T(8,128)(2,1)S(1)}, bf16[1,32,2048]{2,1,0:T(8,128)(2,1)}, u32[]{:S(2)}) %copy-start.2) | copy-done | bytes 131096
  3.9 0.0 copy-start.3
  3.9 0.9 %copy-done.3 = bf16[1,32,2048]{2,1,0:T(8,128)(2,1)S(1)} copy-done((bf16[1,32,2048]{2,1,0:T(8,128)(2,1)S(1)}, bf16[1,32,2048]{2,1,0:T(8,128)(2,1)}, u32[]{:S(2)}) %copy-start.3) | copy-done | bytes 131096
  4.8 0.0 copy-start.4
  4.8 0.8 %copy-done.4 = bf16[1,2048,16]{1,2,0:T(8,128)(2,1)S(1)} copy-done((bf16[1,2048,16]{1,2,0:T(8,128)(2,1)S(1)}, bf16[1,2048,16]{1,2,0:T(8,128)(2,1)}, u32[]{:S(2)}) %copy-start.4) | copy-done | bytes 65560
  5.7 0.0 copy-start.5
  5.7 0.7 %copy-done.5 = s32[1,32,8]{1,2,0:T(8,128)S(1)} copy-done((s32[1,32,8]{1,2,0:T(8,128)S(1)}, s32[1,32,8]{1,2,0:T(8,128)}, u32[]{:S(2)}) %copy-start.5) | copy-done | bytes 1048
  6.3 37.3 %shard_map.85 = (bf16[32,2048]{1,0:T(8,128)(2,1)S(1)}, bf16[384,384]{1,0:T(8,128)(2,1)S(1)}, f32[16,128]{1,0:T(8,128)S(1)}) custom-call(bf16[32,2048]{1,0:T(8,128)(2,1)S(1)} %bitcast.20, bf16[32,2048]{1,0:T(8,128)(2,1)S(1)} %bitcast.21, bf16[16,2048]{1,0:T(8,128)(2,1)S(1)} %bitcast.22, s32[8,32]{1,0:T(8,128)S(1)} %bitcast.23, bf16[384,384]{1,0:T(8,128)(2,1)S(1)} %bitcast.19, ...), custom_call_target="tpu_custom_call" | custom-call | flops 805306368 | bytes 3145728 | tf_op jit(solution)/shard_map/pallas_call | solution.py:356
  43.6 0.7 %copy.12 = bf16[1,32,2048]{2,1,0:T(8,128)(2,1)} copy(bf16[1,32,2048]{2,1,0:T(8,128)(2,1)S(1)} %bitcast.16) | data formatting | bytes 262144
  44.3 0.7 %copy.13 = bf16[1,1,384,384]{3,2,1,0:T(8,128)(2,1)} copy(bf16[1,1,384,384]{3,2,1,0:T(8,128)(2,1)S(1)} %bitcast.15) | data formatting | bytes 589824
  45.0 0.6 %copy.14 = f32[1,128,16]{1,2,0:T(8,128)} copy(f32[1,128,16]{1,2,0:T(8,128)S(1)} %bitcast.17) | data formatting | bytes 16384
Async XLA Ops:
  0.6 1.4 %copy-start = (bf16[1,1,384,2048]{3,2,1,0:T(8,128)(2,1)S(1)}, bf16[1,1,384,2048]{3,2,1,0:T(8,128)(2,1)}, u32[]{:S(2)}) copy-start(bf16[1,1,384,2048]{3,2,1,0:T(8,128)(2,1)} %param.11) | copy-start | bytes 4718596
  2.0 1.0 %copy-start.1 = (bf16[1,1,384,384]{3,2,1,0:T(8,128)(2,1)S(1)}, bf16[1,1,384,384]{3,2,1,0:T(8,128)(2,1)}, u32[]{:S(2)}) copy-start(bf16[1,1,384,384]{3,2,1,0:T(8,128)(2,1)} %param.10) | copy-start | bytes 884740
  3.0 0.9 %copy-start.2 = (bf16[1,32,2048]{2,1,0:T(8,128)(2,1)S(1)}, bf16[1,32,2048]{2,1,0:T(8,128)(2,1)}, u32[]{:S(2)}) copy-start(bf16[1,32,2048]{2,1,0:T(8,128)(2,1)} %param.6) | copy-start | bytes 393220
  3.9 0.9 %copy-start.3 = (bf16[1,32,2048]{2,1,0:T(8,128)(2,1)S(1)}, bf16[1,32,2048]{2,1,0:T(8,128)(2,1)}, u32[]{:S(2)}) copy-start(bf16[1,32,2048]{2,1,0:T(8,128)(2,1)} %param.7) | copy-start | bytes 393220
  4.8 0.8 %copy-start.4 = (bf16[1,2048,16]{1,2,0:T(8,128)(2,1)S(1)}, bf16[1,2048,16]{1,2,0:T(8,128)(2,1)}, u32[]{:S(2)}) copy-start(bf16[1,2048,16]{1,2,0:T(8,128)(2,1)} %param.8) | copy-start | bytes 196612
  5.7 0.7 %copy-start.5 = (s32[1,32,8]{1,2,0:T(8,128)S(1)}, s32[1,32,8]{1,2,0:T(8,128)}, u32[]{:S(2)}) copy-start(s32[1,32,8]{1,2,0:T(8,128)} %param.9) | copy-start | bytes 3076

commit v2 on v1

--- a/solution.py
+++ b/solution.py
@@ -24,7 +24,7 @@
 def kernel(
     sections, n, og, x, rt, ids, hid, w, out_g, out_h, out_r,
     xg, xs, meta, dgb, ogn, rtn, lgn, xv, rtv, idv, hv, wv,
-    gt, sel, hs, u, v, dgo, dg2, lg, outv, hgv, rgv,
+    gt, grow, hvt, sel, hs, u, v, dgo, dg2, lg,
     blk_recv, blk_send, meta_recv, meta_send, slab_recv, slab_send,
     dg_recv, dg_send, sec_recv, sec_send, loc,
 ):
@@ -171,8 +171,6 @@
 
     for q in range(CHUNKS):
         column_sends(a, q, start, own=True)
-    grads_over.start()
-    router_over.start()
 
     own_lane = pl.multiple_of((me * feats) // LANES * LANES, LANES)
     own_slab = pltpu.make_async_copy(x.at[:, pl.ds(own_lane, LANES)], xs.at[me], loc.at[6])
@@ -193,8 +191,11 @@
     meta[me] = dot(marked, place, NN).astype(jnp.bfloat16)
     each_peer(lambda peer: meta_copy(peer).start())
     each_peer(lambda peer: slab_copy(peer).start())
+    grads_over.start()
+    router_over.start()
     for copy in local[3:]:
         copy.wait()
+    hvt[...] = jnp.transpose(hv[...])
 
     def order(k):
         closest = jnp.minimum(a, ROWS_A - 1 - a)
@@ -219,6 +220,7 @@
                 total = total + meta[j * per_tile + i].astype(jnp.float32)
             gt[j] = total
             mine = jnp.sum(jnp.where(erow == me, total, 0.0), axis=0, keepdims=True)
+            grow[j : j + 1, :] = jnp.maximum(mine, 0.0)
             taken = jnp.where(mine >= 0.0, 1.0, 0.0)
             many = jnp.broadcast_to(taken, (16, LANES)).astype(jnp.bfloat16)
             rank = dot(many, ahead, NN)[0:1, :].astype(jnp.int32)
@@ -226,53 +228,92 @@
             slot = jnp.where(mine >= 0.0, slot, -1)
             hot = jnp.where(slot_row == slot, 1.0, 0.0).astype(jnp.bfloat16)
             sel[:, j * LANES : (j + 1) * LANES] = hot
-            hs[j] = dot(hv[...], hot, TN)
-
-    def step(k, carry):
-        @pl.when(k < ROWS_A - 1)
-        def _():
-            g = order(k + 1)
-            idx = (g * nb + b) * 2 + c
-            for q in range(CHUNKS):
-                block_copy(idx, q, sib, SIB).wait_recv()
-                column_sends(g, q, start)
-
-        g = order(k)
-        for j in range(1, nb):
-            b2 = lax.rem(b + j, nb)
-            idx = (g * nb + b2) * 2 + c
-            for q in range(CHUNKS):
-                block_copy(idx, q, sib, SIB).wait_recv()
-                cross_sends(g, b2, q, start)
-        for b2 in range(nb):
-            idx = (g * nb + b2) * 2 + 1 - c
-            for q in range(CHUNKS):
-                block_copy(idx, q, sib, SIB).wait_recv()
-
-        @pl.when(k == ROWS_A - 2)
-        def _():
-            slots_of_expert()
-
+            hs[j] = dot(hvt[...], hot, NN)
+
+    def products(g):
         for i in range(tiles_per_group):
             t = g * tiles_per_group + i
             u[t] = dot(
                 wv[...], xg[pl.ds(t * per_tile, per_tile)].reshape(LANES, d_model), NT
             )
+
+    def gradients(g):
+        for i in range(tiles_per_group):
+            t = g * tiles_per_group + i
+            lanes = pl.ds(pl.multiple_of(t * LANES, LANES), LANES)
+            dgo[pl.ds(t, 1), :] = jnp.sum(u[t] * hs[t], axis=0, keepdims=True)
+            v[:, lanes] = (u[t] * grow[pl.ds(t, 1), :]).astype(jnp.bfloat16)
+
+    def step(k, carry):
+        for q in range(CHUNKS):
+            for g, there in ((a - k - 1, a - k - 1 >= 0), (a + k + 1, a + k + 1 < ROWS_A)):
+                @pl.when(there)
+                def _():
+                    block_copy((g * nb + b) * 2 + c, q, sib, SIB).wait_recv()
+                    column_sends(g, q, start)
+
+        @pl.when(k < ROWS_A)
+        def _():
+            g = order(k)
+            for j in range(1, nb):
+                b2 = lax.rem(b + j, nb)
+                for q in range(CHUNKS):
+                    block_copy((g * nb + b2) * 2 + c, q, sib, SIB).wait_recv()
+                    cross_sends(g, b2, q, start)
+
+        @pl.when(k == 2)
+        def _():
+            slots_of_expert()
+
+        @pl.when(k > 0)
+        def _():
+            g = order(k - 1)
+            for b2 in range(nb):
+                for q in range(CHUNKS):
+                    block_copy((g * nb + b2) * 2 + 1 - c, q, sib, SIB).wait_recv()
+            products(g)
+
+        @pl.when(k == 2)
+        def _():
+            gradients(order(0))
+
+        @pl.when(k >= 2)
+        def _():
+            gradients(order(k - 1))
+
         return carry
 
-    lax.fori_loop(0, ROWS_A, step, 0)
-
-    for j in range(tiles):
-        dgo[j : j + 1, :] = jnp.sum(u[j] * hs[j], axis=0, keepdims=True)
+    lax.fori_loop(0, ROWS_A + 1, step, 0)
+
     each_peer(lambda peer: dg_copy(peer).start())
 
-    erow = lax.broadcasted_iota(jnp.int32, (experts, LANES), 0)
-    for j in range(tiles):
-        mine = jnp.sum(jnp.where(erow == me, gt[j], 0.0), axis=0, keepdims=True)
-        v[:, j * LANES : (j + 1) * LANES] = (u[j] * jnp.maximum(mine, 0.0)).astype(jnp.bfloat16)
-    hgv[...] = dot(sel[...], v[...], NT).astype(jnp.bfloat16)
-    hidden_out = pltpu.make_async_copy(hgv, out_h, loc.at[7])
-    hidden_out.start()
+    out_h[...] = dot(sel[...], v[...], NT).astype(jnp.bfloat16)
+
+    for q in range(CHUNKS):
+        column_sends(a, q, finish, own=True)
+
+    def drain(k, carry):
+        g = order(k)
+
+        @pl.when(k > 0)
+        def _():
+            for q in range(CHUNKS):
+                column_sends(g, q, finish)
+
+        for j in range(1, nb):
+            for q in range(CHUNKS):
+                cross_sends(g, lax.rem(b + j, nb), q, finish)
+        return carry
+
+    lax.fori_loop(0, ROWS_A, drain, 0)
+
+    def sent(peer):
+        meta_copy(peer).wait_send()
+        slab_copy(peer).wait_send()
+
+    each_peer(sent)
+    grads_over.wait_send()
+    router_over.wait_send()
 
     own_slab.wait()
     each_peer(lambda peer: await_from(peer, xs.at[peer], slab_recv.at[peer]))
@@ -299,46 +340,25 @@
     if feats < LANES:
         shift = lax.rem(LANES - lax.rem(me * feats, LANES), LANES)
         part = pltpu.roll(part, shift, 1)[:, :feats]
-    rgv[...] = part
-    router_out = pltpu.make_async_copy(rgv, out_r, loc.at[8])
-    router_out.start()
+    out_r[...] = part
 
     logit_over.wait_recv()
     mine = dot(place, lgn[...], NT).astype(jnp.bfloat16)
-    outv[...] = (ogn[...].astype(jnp.float32) + dot(mine, rtn[...], NN)).astype(jnp.bfloat16)
-    grads_out = pltpu.make_async_copy(outv, out_g, loc.at[9])
-    grads_out.start()
-
-    for q in range(CHUNKS):
-        column_sends(a, q, finish, own=True)
-
-    def drain(k, carry):
-        g = order(k)
-
-        @pl.when(k > 0)
-        def _():
-            for q in range(CHUNKS):
-                column_sends(g, q, finish)
-
-        for j in range(1, nb):
-            for q in range(CHUNKS):
-                cross_sends(g, lax.rem(b + j, nb), q, finish)
-        return carry
-
-    lax.fori_loop(0, ROWS_A, drain, 0)
-
-    def sent(peer):
-        meta_copy(peer).wait_send()
-        slab_copy(peer).wait_send()
-        dg_copy(peer).wait_send()
-
-    each_peer(sent)
-    grads_over.wait_send()
-    router_over.wait_send()
+    out_g[...] = (ogn[...].astype(jnp.float32) + dot(mine, rtn[...], NN)).astype(jnp.bfloat16)
+    each_peer(lambda peer: dg_copy(peer).wait_send())
     logit_over.wait_send()
-    hidden_out.wait()
-    router_out.wait()
-    grads_out.wait()
+
+
+def write_out(grads, hidden, router, out_g, out_h, out_r, sem):
+    copies = [
+        pltpu.make_async_copy(grads, out_g, sem.at[0]),
+        pltpu.make_async_copy(hidden, out_h, sem.at[1]),
+        pltpu.make_async_copy(router, out_r, sem.at[2]),
+    ]
+    for copy in copies:
+        copy.start()
+    for copy in copies:
+        copy.wait()
 
 
 def shards(sections, n, out_grad, layer_input, router_weight, expert_ids, hidden_act, down_weight):
@@ -352,16 +372,18 @@
     tiles = total // LANES
     bf16, f32 = jnp.bfloat16, jnp.float32
     dma = pltpu.SemaphoreType.DMA
-    hbm = pl.BlockSpec(memory_space=pl.ANY)
-    grads, hidden, router = pl.pallas_call(
+    hbm = pl.BlockSpec(memory_space=pltpu.HBM)
+    vmem = pl.BlockSpec(memory_space=pltpu.VMEM)
+    results = (
+        jax.ShapeDtypeStruct((tokens, d_model), bf16),
+        jax.ShapeDtypeStruct((slots, f_dim), bf16),
+        jax.ShapeDtypeStruct((experts, feats), f32),
+    )
+    held = pl.pallas_call(
         functools.partial(kernel, sections, n),
-        out_shape=(
-            jax.ShapeDtypeStruct((tokens, d_model), bf16),
-            jax.ShapeDtypeStruct((slots, f_dim), bf16),
-            jax.ShapeDtypeStruct((experts, feats), f32),
-        ),
+        out_shape=results,
         in_specs=[hbm] * 6,
-        out_specs=(hbm,) * 3,
+        out_specs=(vmem,) * 3,
         scratch_shapes=[
             pltpu.VMEM((n, tokens, d_model), bf16),
             pltpu.VMEM((n, tokens, LANES), bf16),
@@ -376,6 +398,8 @@
             pltpu.VMEM((slots, f_dim), bf16),
             pltpu.VMEM((f_dim, d_model), bf16),
             pltpu.VMEM((tiles, experts, LANES), f32),
+            pltpu.VMEM((tiles, LANES), f32),
+            pltpu.VMEM((f_dim, slots), bf16),
             pltpu.VMEM((slots, total), bf16),
             pltpu.VMEM((tiles, f_dim, LANES), f32),
             pltpu.VMEM((tiles, f_dim, LANES), f32),
@@ -383,9 +407,6 @@
             pltpu.VMEM((tiles, LANES), f32),
             pltpu.VMEM((tiles, experts, LANES), f32),
             pltpu.VMEM((tiles, experts, LANES), bf16),
-            pltpu.VMEM((tokens, d_model), bf16),
-            pltpu.VMEM((slots, f_dim), bf16),
-            pltpu.VMEM((experts, feats), f32),
             dma((n, CHUNKS)),
             dma((n, CHUNKS, 5)),
             dma((n,)),
@@ -396,7 +417,7 @@
             dma((n,)),
             dma((3,)),
             dma((3,)),
-            dma((10,)),
+            dma((7,)),
         ],
         compiler_params=pltpu.CompilerParams(
             collective_id=0, has_side_effects=True, vmem_limit_bytes=48 * 2**20
@@ -404,7 +425,14 @@
         cost_estimate=pl.CostEstimate(
             flops=2 * total * d_model * f_dim, bytes_accessed=4 * f_dim * d_model, transcendentals=0
         ),
-    )(og, x, rt, ids, hid, w)
+    )(*(pltpu.with_memory_space_constraint(p, pltpu.HBM) for p in (og, x, rt, ids, hid, w)))
+    grads, hidden, router = pl.pallas_call(
+        write_out,
+        out_shape=results,
+        in_specs=[vmem] * 3,
+        out_specs=(hbm,) * 3,
+        scratch_shapes=[dma((3,))],
+    )(*held)
     return (grads[None], hidden[None, None], router.T[None])
 
 

time: 45.9 us -> 40.9 us (0.89)
  local copies, waits for them, and re-layouts: 7.66 us -> 1.94 us
  Pallas kernels: 37.3 us -> 38.1 us
    unnamed x15 -> x6, local copies, waits for them, and re-layouts: 7.66 us -> 1.94 us
    pallas_call x1 -> x2, Pallas kernels: 37.3 us -> 38.1 us  [the longest x1 36.3 us: shards(): pl.pallas_call(functools.partial(kernel, sections, n), out_shape=results,...]
where the time goes in v2:
time: 40.9 us; the launch traced here: 40.7 us
  Pallas kernels  38.1 us (93%)
  local copies, waits for them, and re-layouts  1.94 us (5%)
  between operations  0.65 us (2%)
    pallas_call x1, Pallas kernels, shards(): pl.pallas_call(functools.partial(kernel, sections, n), out_shape=results,...  36.3 us
    unnamed x6, local copies, waits for them, and re-layouts  1.94 us
    pallas_call x1, Pallas kernels, shards(): pl.pallas_call(write_out, out_shape=results, in_specs=[vmem] * 3, out_spe...  1.78 us

profile of v2, /device:TPU:0, one launch (start us, length us, event | category | flops | bytes accessed | tf_op | source)
XLA Modules:
  0.0 40.7 jit_solution(1221501795298855918)
XLA Ops:
  0.6 36.3 %shard_map.85 = (bf16[32,2048]{1,0:T(8,128)(2,1)S(1)}, bf16[384,384]{1,0:T(8,128)(2,1)S(1)}, f32[16,128]{1,0:T(8,128)S(1)}) custom-call(bf16[32,2048]{1,0:T(8,128)(2,1)} %bitcast.18, bf16[32,2048]{1,0:T(8,128)(2,1)} %bitcast.19, bf16[16,2048]{1,0:T(8,128)(2,1)} %bitcast.21, s32[8,32]{1,0:T(8,128)} %bitcast.23, bf16[384,384]{1,0:T(8,128)(2,1)} %bitcast.16, ...), custom_call_target="tpu_custom_call" | custom-call | flops 805306368 | bytes 3145728 | tf_op jit(solution)/shard_map/pallas_call | solution.py:382
  37.0 0.0 copy-start
  37.0 0.7 %copy-done = bf16[384,384]{1,0:T(8,128)(2,1)} copy-done((bf16[384,384]{1,0:T(8,128)(2,1)}, bf16[384,384]{1,0:T(8,128)(2,1)S(1)}, u32[]{:S(2)}) %copy-start) | copy-done | bytes 294936
  37.7 0.0 copy-start.1
  37.7 0.6 %copy-done.1 = bf16[32,2048]{1,0:T(8,128)(2,1)} copy-done((bf16[32,2048]{1,0:T(8,128)(2,1)}, bf16[32,2048]{1,0:T(8,128)(2,1)S(1)}, u32[]{:S(2)}) %copy-start.1) | copy-done | bytes 131096
  38.3 0.0 copy-start.2
  38.3 0.6 %copy-done.2 = f32[16,128]{1,0:T(8,128)} copy-done((f32[16,128]{1,0:T(8,128)}, f32[16,128]{1,0:T(8,128)S(1)}, u32[]{:S(2)}) %copy-start.2) | copy-done | bytes 8216
  38.9 1.8 %shard_map.86 = (bf16[32,2048]{1,0:T(8,128)(2,1)}, bf16[384,384]{1,0:T(8,128)(2,1)}, f32[16,128]{1,0:T(8,128)}) custom-call(bf16[32,2048]{1,0:T(8,128)(2,1)} %copy-done.1, bf16[384,384]{1,0:T(8,128)(2,1)} %copy-done, f32[16,128]{1,0:T(8,128)} %copy-done.2), custom_call_target="tpu_custom_call" | custom-call | tf_op jit(solution)/shard_map/pallas_call | solution.py:429
Async XLA Ops:
  37.0 0.7 %copy-start = (bf16[384,384]{1,0:T(8,128)(2,1)}, bf16[384,384]{1,0:T(8,128)(2,1)S(1)}, u32[]{:S(2)}) copy-start(bf16[384,384]{1,0:T(8,128)(2,1)S(1)} %get-tuple-element.10.hidden) | copy-start | bytes 884740
  37.7 0.6 %copy-start.1 = (bf16[32,2048]{1,0:T(8,128)(2,1)}, bf16[32,2048]{1,0:T(8,128)(2,1)S(1)}, u32[]{:S(2)}) copy-start(bf16[32,2048]{1,0:T(8,128)(2,1)S(1)} %get-tuple-element.9.grads) | copy-start | bytes 393220
  38.3 0.6 %copy-start.2 = (f32[16,128]{1,0:T(8,128)}, f32[16,128]{1,0:T(8,128)S(1)}, u32[]{:S(2)}) copy-start(f32[16,128]{1,0:T(8,128)S(1)} %get-tuple-element.11.router) | copy-start | bytes 24580

commit v3 on v2

--- a/solution.py
+++ b/solution.py
@@ -51,6 +51,8 @@
     tile = me // per_tile
     offset = lax.rem(me, per_tile) * tokens
 
+    ring = lambda i: jnp.where(i >= n, i - n, i)
+
     local = [
         pltpu.make_async_copy(x, xv, loc.at[0]),
         pltpu.make_async_copy(rt, rtv, loc.at[1]),
@@ -66,7 +68,7 @@
 
     def greet(d, carry):
         pl.semaphore_signal(
-            barrier, inc=1, device_id={"expert": lax.rem(me + d, n)}, device_id_type=MESH
+            barrier, inc=1, device_id={"expert": ring(me + d)}, device_id_type=MESH
         )
         return carry
 
@@ -87,8 +89,17 @@
             device_id_type=MESH,
         )
 
+    def at_end(g):
+        return jnp.logical_or(g == 0, g == ROWS_A - 1)
+
+    def crossed_early(g, q):
+        if nb > 2 or q > 0:
+            return jnp.logical_and(g == a, g != a)
+        return jnp.logical_and(at_end(g), g != a)
+
     def column_sends(g, q, do, own=False):
         idx = (g * nb + b) * 2 + c
+        crosses = jnp.logical_not(crossed_early(g, q))
 
         @pl.when(jnp.logical_and(g <= a, a < ROWS_A - 1))
         def _():
@@ -98,11 +109,11 @@
         def _():
             do(block_copy(idx, q, me - 2 * nb, A_DOWN, own))
 
-        @pl.when(b < nb - 1)
+        @pl.when(jnp.logical_and(crosses, b < nb - 1))
         def _():
             do(block_copy(idx, q, me + 2, B_NEXT, own))
 
-        @pl.when(b > 0)
+        @pl.when(jnp.logical_and(crosses, b > 0))
         def _():
             do(block_copy(idx, q, me - 2, B_PREV, own))
 
@@ -119,6 +130,15 @@
             def _():
                 do(block_copy(idx, q, me - 2, B_PREV))
 
+        elif q == 0:
+            @pl.when(jnp.logical_and(at_end(g), jnp.logical_and(g <= a, a < ROWS_A - 1)))
+            def _():
+                do(block_copy(idx, q, me + 2 * nb, A_UP))
+
+            @pl.when(jnp.logical_and(at_end(g), jnp.logical_and(g >= a, a > 0)))
+            def _():
+                do(block_copy(idx, q, me - 2 * nb, A_DOWN))
+
         do(block_copy(idx, q, sib, SIB))
 
     def section_copy(i, src, dst):
@@ -161,7 +181,7 @@
 
     def each_peer(fn):
         def step(d, carry):
-            fn(lax.rem(me + d, n))
+            fn(ring(me + d))
             return carry
 
         lax.fori_loop(1, n, step, 0)
@@ -244,6 +264,16 @@
             dgo[pl.ds(t, 1), :] = jnp.sum(u[t] * hs[t], axis=0, keepdims=True)
             v[:, lanes] = (u[t] * grow[pl.ds(t, 1), :]).astype(jnp.bfloat16)
 
+    def from_sibling(g):
+        for b2 in range(nb):
+            for q in range(CHUNKS):
+                block_copy((g * nb + b2) * 2 + 1 - c, q, sib, SIB).wait_recv()
+        products(g)
+
+    def sent(peer):
+        meta_copy(peer).wait_send()
+        slab_copy(peer).wait_send()
+
     def step(k, carry):
         for q in range(CHUNKS):
             for g, there in ((a - k - 1, a - k - 1 >= 0), (a + k + 1, a + k + 1 < ROWS_A)):
@@ -252,68 +282,50 @@
                     block_copy((g * nb + b) * 2 + c, q, sib, SIB).wait_recv()
                     column_sends(g, q, start)
 
-        @pl.when(k < ROWS_A)
-        def _():
-            g = order(k)
-            for j in range(1, nb):
-                b2 = lax.rem(b + j, nb)
-                for q in range(CHUNKS):
+        if nb == 2:
+            for g, there in ((a - k - 1, a - k - 1 >= 0), (a + k + 1, a + k + 1 < ROWS_A)):
+                @pl.when(jnp.logical_and(there, at_end(g)))
+                def _():
+                    block_copy((g * nb + 1 - b) * 2 + c, 0, sib, SIB).wait_recv()
+                    cross_sends(g, 1 - b, 0, start)
+
+        @pl.when(jnp.logical_and(k > 0, k < ROWS_A))
+        def _():
+            from_sibling(order(k - 1))
+
+        @pl.when(k == 2)
+        def _():
+            slots_of_expert()
+            gradients(order(0))
+
+        @pl.when(jnp.logical_and(k >= 2, k < ROWS_A))
+        def _():
+            gradients(order(k - 1))
+
+        @pl.when(k == ROWS_A - 1)
+        def _():
+            for q in range(CHUNKS):
+                column_sends(a, q, finish, own=True)
+            each_peer(sent)
+
+        g = order(k)
+        for j in range(1, nb):
+            b2 = lax.rem(b + j, nb)
+            for q in range(CHUNKS):
+                @pl.when(jnp.logical_not(crossed_early(g, q)))
+                def _():
                     block_copy((g * nb + b2) * 2 + c, q, sib, SIB).wait_recv()
                     cross_sends(g, b2, q, start)
 
-        @pl.when(k == 2)
-        def _():
-            slots_of_expert()
-
-        @pl.when(k > 0)
-        def _():
-            g = order(k - 1)
-            for b2 in range(nb):
-                for q in range(CHUNKS):
-                    block_copy((g * nb + b2) * 2 + 1 - c, q, sib, SIB).wait_recv()
-            products(g)
-
-        @pl.when(k == 2)
-        def _():
-            gradients(order(0))
-
-        @pl.when(k >= 2)
-        def _():
-            gradients(order(k - 1))
-
         return carry
 
-    lax.fori_loop(0, ROWS_A + 1, step, 0)
+    lax.fori_loop(0, ROWS_A, step, 0)
+    from_sibling(order(ROWS_A - 1))
+    gradients(order(ROWS_A - 1))
 
     each_peer(lambda peer: dg_copy(peer).start())
 
     out_h[...] = dot(sel[...], v[...], NT).astype(jnp.bfloat16)
-
-    for q in range(CHUNKS):
-        column_sends(a, q, finish, own=True)
-
-    def drain(k, carry):
-        g = order(k)
-
-        @pl.when(k > 0)
-        def _():
-            for q in range(CHUNKS):
-                column_sends(g, q, finish)
-
-        for j in range(1, nb):
-            for q in range(CHUNKS):
-                cross_sends(g, lax.rem(b + j, nb), q, finish)
-        return carry
-
-    lax.fori_loop(0, ROWS_A, drain, 0)
-
-    def sent(peer):
-        meta_copy(peer).wait_send()
-        slab_copy(peer).wait_send()
-
-    each_peer(sent)
-    grads_over.wait_send()
-    router_over.wait_send()
 
     own_slab.wait()
     each_peer(lambda peer: await_from(peer, xs.at[peer], slab_recv.at[peer]))
@@ -341,6 +353,23 @@
         shift = lax.rem(LANES - lax.rem(me * feats, LANES), LANES)
         part = pltpu.roll(part, shift, 1)[:, :feats]
     out_r[...] = part
+
+    def drain(k, carry):
+        g = order(k)
+
+        @pl.when(k > 0)
+        def _():
+            for q in range(CHUNKS):
+                column_sends(g, q, finish)
+
+        for j in range(1, nb):
+            for q in range(CHUNKS):
+                cross_sends(g, lax.rem(b + j, nb), q, finish)
+        return carry
+
+    lax.fori_loop(0, ROWS_A, drain, 0)
+    grads_over.wait_send()
+    router_over.wait_send()
 
     logit_over.wait_recv()
     mine = dot(place, lgn[...], NT).astype(jnp.bfloat16)
@@ -381,7 +410,7 @@
     )
     held = pl.pallas_call(
         functools.partial(kernel, sections, n),
-        out_shape=results,
+        out_shape=tuple(pltpu.VMEM(r.shape, r.dtype) for r in results),
         in_specs=[hbm] * 6,
         out_specs=(vmem,) * 3,
         scratch_shapes=[

time: 40.9 us -> 42.8 us (1.046)
  Pallas kernels: 38.1 us -> 40 us
    pallas_call x1, Pallas kernels: 36.3 us -> 38.3 us  [shards(): pl.pallas_call(functools.partial(kernel, sections, n), out_shape=tuple((p...]
where the time goes in v3:
time: 42.8 us; the launch traced here: 42.6 us
  Pallas kernels  40 us (93%)
  local copies, waits for them, and re-layouts  1.94 us (5%)
  between operations  0.65 us (2%)
    pallas_call x1, Pallas kernels, shards(): pl.pallas_call(functools.partial(kernel, sections, n), out_shape=tuple((p...  38.3 us
    unnamed x6, local copies, waits for them, and re-layouts  1.94 us
    pallas_call x1, Pallas kernels, shards(): pl.pallas_call(write_out, out_shape=results, in_specs=[vmem] * 3, out_spe...  1.78 us

profile of v3, /device:TPU:0, one launch (start us, length us, event | category | flops | bytes accessed | tf_op | source)
XLA Modules:
  0.0 42.6 jit_solution(3448828539701015516)
XLA Ops:
  0.6 38.3 %shard_map.85 = (bf16[32,2048]{1,0:T(8,128)(2,1)S(1)}, bf16[384,384]{1,0:T(8,128)(2,1)S(1)}, f32[16,128]{1,0:T(8,128)S(1)}) custom-call(bf16[32,2048]{1,0:T(8,128)(2,1)} %bitcast.18, bf16[32,2048]{1,0:T(8,128)(2,1)} %bitcast.19, bf16[16,2048]{1,0:T(8,128)(2,1)} %bitcast.21, s32[8,32]{1,0:T(8,128)} %bitcast.23, bf16[384,384]{1,0:T(8,128)(2,1)} %bitcast.16, ...), custom_call_target="tpu_custom_call" | custom-call | flops 805306368 | bytes 3145728 | tf_op jit(solution)/shard_map/pallas_call | solution.py:411
  38.9 0.0 copy-start
  38.9 0.7 %copy-done = bf16[384,384]{1,0:T(8,128)(2,1)} copy-done((bf16[384,384]{1,0:T(8,128)(2,1)}, bf16[384,384]{1,0:T(8,128)(2,1)S(1)}, u32[]{:S(2)}) %copy-start) | copy-done | bytes 294936
  39.6 0.0 copy-start.1
  39.6 0.6 %copy-done.1 = bf16[32,2048]{1,0:T(8,128)(2,1)} copy-done((bf16[32,2048]{1,0:T(8,128)(2,1)}, bf16[32,2048]{1,0:T(8,128)(2,1)S(1)}, u32[]{:S(2)}) %copy-start.1) | copy-done | bytes 131096
  40.3 0.0 copy-start.2
  40.3 0.6 %copy-done.2 = f32[16,128]{1,0:T(8,128)} copy-done((f32[16,128]{1,0:T(8,128)}, f32[16,128]{1,0:T(8,128)S(1)}, u32[]{:S(2)}) %copy-start.2) | copy-done | bytes 8216
  40.9 1.8 %shard_map.86 = (bf16[32,2048]{1,0:T(8,128)(2,1)}, bf16[384,384]{1,0:T(8,128)(2,1)}, f32[16,128]{1,0:T(8,128)}) custom-call(bf16[32,2048]{1,0:T(8,128)(2,1)} %copy-done.1, bf16[384,384]{1,0:T(8,128)(2,1)} %copy-done, f32[16,128]{1,0:T(8,128)} %copy-done.2), custom_call_target="tpu_custom_call" | custom-call | tf_op jit(solution)/shard_map/pallas_call | solution.py:458
Async XLA Ops:
  38.9 0.7 %copy-start = (bf16[384,384]{1,0:T(8,128)(2,1)}, bf16[384,384]{1,0:T(8,128)(2,1)S(1)}, u32[]{:S(2)}) copy-start(bf16[384,384]{1,0:T(8,128)(2,1)S(1)} %get-tuple-element.10.hidden) | copy-start | bytes 884740
  39.6 0.6 %copy-start.1 = (bf16[32,2048]{1,0:T(8,128)(2,1)}, bf16[32,2048]{1,0:T(8,128)(2,1)S(1)}, u32[]{:S(2)}) copy-start(bf16[32,2048]{1,0:T(8,128)(2,1)S(1)} %get-tuple-element.9.grads) | copy-start | bytes 393220
  40.3 0.6 %copy-start.2 = (f32[16,128]{1,0:T(8,128)}, f32[16,128]{1,0:T(8,128)S(1)}, u32[]{:S(2)}) copy-start(f32[16,128]{1,0:T(8,128)S(1)} %get-tuple-element.11.router) | copy-start | bytes 24580

commit v4 on v2

--- a/solution.py
+++ b/solution.py
@@ -13,7 +13,7 @@
 NN = (((1,), (0,)), ((), ()))
 LANES = 128
 ROWS_A = 4
-CHUNKS = 2
+CHUNKS = 1
 A_UP, A_DOWN, B_NEXT, B_PREV, SIB = range(5)
 
 
@@ -23,10 +23,9 @@
 
 def kernel(
     sections, n, og, x, rt, ids, hid, w, out_g, out_h, out_r,
-    xg, xs, meta, dgb, ogn, rtn, lgn, xv, rtv, idv, hv, wv,
-    gt, grow, hvt, sel, hs, u, v, dgo, dg2, lg,
-    blk_recv, blk_send, meta_recv, meta_send, slab_recv, slab_send,
-    dg_recv, dg_send, sec_recv, sec_send, loc,
+    xg, xs, stage, dgb, ogn, rtn, lgn, xv, rtv, idv, hv, wv,
+    gt, grow, hvt, sel, hs, u, v, dgo, dg2, lg, outv, hgv, rgv,
+    blk_recv, blk_send, sib_recv, peer_recv, peer_send, sec_recv, sec_send, loc,
 ):
     tokens, d_model = og.shape
     topk = ids.shape[0]
@@ -51,6 +50,8 @@
     tile = me // per_tile
     offset = lax.rem(me, per_tile) * tokens
 
+    ring = lambda i: jnp.where(i >= n, i - n, i)
+
     local = [
         pltpu.make_async_copy(x, xv, loc.at[0]),
         pltpu.make_async_copy(rt, rtv, loc.at[1]),
@@ -66,7 +67,7 @@
 
     def greet(d, carry):
         pl.semaphore_signal(
-            barrier, inc=1, device_id={"expert": lax.rem(me + d, n)}, device_id_type=MESH
+            barrier, inc=1, device_id={"expert": ring(me + d)}, device_id_type=MESH
         )
         return carry
 
@@ -76,13 +77,22 @@
         pl.semaphore_signal(barrier, inc=1, device_id={"section": other}, device_id_type=MESH)
     pl.semaphore_wait(barrier, n - 1 + len(near))
 
+    start = lambda copy: copy.start()
+    finish = lambda copy: copy.wait_send()
+
+    def whole(ref, sem):
+        return pltpu.make_async_remote_copy(
+            src_ref=ref, dst_ref=ref, send_sem=sem, recv_sem=sem,
+            device_id={"expert": sib}, device_id_type=MESH,
+        )
+
     def block_copy(idx, q, target, way, own=False):
         part = pl.ds(q * rows, rows)
         return pltpu.make_async_remote_copy(
             src_ref=og.at[part] if own else xg.at[idx, part],
             dst_ref=xg.at[idx, part],
-            send_sem=blk_send.at[idx, q, way],
-            recv_sem=blk_recv.at[idx, q],
+            send_sem=peer_send.at[2] if way == SIB else blk_send.at[idx, q, way],
+            recv_sem=sib_recv.at[idx // (2 * nb)] if way == SIB else blk_recv.at[idx, q],
             device_id={"expert": target},
             device_id_type=MESH,
         )
@@ -106,7 +116,8 @@
         def _():
             do(block_copy(idx, q, me - 2, B_PREV, own))
 
-        do(block_copy(idx, q, sib, SIB, own))
+        if do is start:
+            do(block_copy(idx, q, sib, SIB, own))
 
     def cross_sends(g, b2, q, do):
         idx = (g * nb + b2) * 2 + c
@@ -119,7 +130,8 @@
             def _():
                 do(block_copy(idx, q, me - 2, B_PREV))
 
-        do(block_copy(idx, q, sib, SIB))
+        if do is start:
+            do(block_copy(idx, q, sib, SIB))
 
     def section_copy(i, src, dst):
         return pltpu.make_async_remote_copy(
@@ -131,50 +143,31 @@
     router_over = section_copy(1, rt, rtn)
     logit_over = section_copy(2, lg.at[tile], lgn)
 
-    def slab_copy(peer):
-        lane = pl.multiple_of((peer * feats) // LANES * LANES, LANES)
+    def mixed_copy(peer):
         return pltpu.make_async_remote_copy(
-            src_ref=x.at[:, pl.ds(lane, LANES)], dst_ref=xs.at[me],
-            send_sem=slab_send.at[peer], recv_sem=slab_recv.at[me],
-            device_id={"expert": peer}, device_id_type=MESH,
-        )
-
-    def meta_copy(peer):
-        return pltpu.make_async_remote_copy(
-            src_ref=meta.at[me], dst_ref=meta.at[me],
-            send_sem=meta_send.at[peer], recv_sem=meta_recv.at[me],
+            src_ref=stage.at[peer], dst_ref=xs.at[me],
+            send_sem=peer_send.at[0], recv_sem=peer_recv.at[0],
             device_id={"expert": peer}, device_id_type=MESH,
         )
 
     def dg_copy(peer):
         return pltpu.make_async_remote_copy(
             src_ref=dgo, dst_ref=dgb.at[me],
-            send_sem=dg_send.at[peer], recv_sem=dg_recv.at[me],
+            send_sem=peer_send.at[1], recv_sem=peer_recv.at[1],
             device_id={"expert": peer}, device_id_type=MESH,
         )
-
-    def await_from(peer, dst, sem):
-        pltpu.make_async_remote_copy(
-            src_ref=dst, dst_ref=dst, send_sem=sem, recv_sem=sem,
-            device_id={"expert": peer}, device_id_type=MESH,
-        ).wait_recv()
 
     def each_peer(fn):
         def step(d, carry):
-            fn(lax.rem(me + d, n))
+            fn(ring(me + d))
             return carry
 
         lax.fori_loop(1, n, step, 0)
 
-    start = lambda copy: copy.start()
-    finish = lambda copy: copy.wait_send()
 
     for q in range(CHUNKS):
         column_sends(a, q, start, own=True)
 
-    own_lane = pl.multiple_of((me * feats) // LANES * LANES, LANES)
-    own_slab = pltpu.make_async_copy(x.at[:, pl.ds(own_lane, LANES)], xs.at[me], loc.at[6])
-    own_slab.start()
     for copy in local[:3]:
         copy.wait()
     logits = dot(rtv[...], xv[...], NT)
@@ -188,9 +181,13 @@
     token_of = lax.broadcasted_iota(jnp.int32, (tokens, LANES), 0)
     lane_of = lax.broadcasted_iota(jnp.int32, (tokens, LANES), 1)
     place = jnp.where(lane_of == token_of + offset, 1.0, 0.0).astype(jnp.bfloat16)
-    meta[me] = dot(marked, place, NN).astype(jnp.bfloat16)
-    each_peer(lambda peer: meta_copy(peer).start())
-    each_peer(lambda peer: slab_copy(peer).start())
+    mark = dot(marked, place, NN).astype(jnp.bfloat16)
+    for peer in range(n):
+        lane = peer * feats // LANES * LANES
+        stage[peer, :tokens, :] = xv[:, lane : lane + LANES]
+        stage[peer, tokens:, :] = mark
+    xs[me] = stage[me]
+    each_peer(lambda peer: mixed_copy(peer).start())
     grads_over.start()
     router_over.start()
     for copy in local[3:]:
@@ -205,7 +202,7 @@
         return jnp.where(k <= 2 * closest, both, rest)
 
     def slots_of_expert():
-        each_peer(lambda peer: await_from(peer, meta.at[peer], meta_recv.at[peer]))
+        whole(xs.at[pl.ds(0, n - 1)], peer_recv.at[0]).wait_recv()
         erow = lax.broadcasted_iota(jnp.int32, (experts, LANES), 0)
         t_from = lax.broadcasted_iota(jnp.int32, (LANES, LANES), 0)
         t_to = lax.broadcasted_iota(jnp.int32, (LANES, LANES), 1)
@@ -215,9 +212,9 @@
         lane_block = lax.broadcasted_iota(jnp.int32, (1, LANES), 1) // tokens
         slot_row = lax.broadcasted_iota(jnp.int32, (slots, LANES), 0)
         for j in range(tiles):
-            total = meta[j * per_tile].astype(jnp.float32)
+            total = xs[j * per_tile, tokens:, :].astype(jnp.float32)
             for i in range(1, per_tile):
-                total = total + meta[j * per_tile + i].astype(jnp.float32)
+                total = total + xs[j * per_tile + i, tokens:, :].astype(jnp.float32)
             gt[j] = total
             mine = jnp.sum(jnp.where(erow == me, total, 0.0), axis=0, keepdims=True)
             grow[j : j + 1, :] = jnp.maximum(mine, 0.0)
@@ -249,7 +246,7 @@
             for g, there in ((a - k - 1, a - k - 1 >= 0), (a + k + 1, a + k + 1 < ROWS_A)):
                 @pl.when(there)
                 def _():
-                    block_copy((g * nb + b) * 2 + c, q, sib, SIB).wait_recv()
+                    block_copy((g * nb + b) * 2 + c, q, sib, A_UP).wait_recv()
                     column_sends(g, q, start)
 
         @pl.when(k < ROWS_A)
@@ -258,7 +255,7 @@
             for j in range(1, nb):
                 b2 = lax.rem(b + j, nb)
                 for q in range(CHUNKS):
-                    block_copy((g * nb + b2) * 2 + c, q, sib, SIB).wait_recv()
+                    block_copy((g * nb + b2) * 2 + c, q, sib, A_UP).wait_recv()
                     cross_sends(g, b2, q, start)
 
         @pl.when(k == 2)
@@ -268,9 +265,7 @@
         @pl.when(k > 0)
         def _():
             g = order(k - 1)
-            for b2 in range(nb):
-                for q in range(CHUNKS):
-                    block_copy((g * nb + b2) * 2 + 1 - c, q, sib, SIB).wait_recv()
+            whole(xg.at[pl.ds(g * 2 * nb, nb)], sib_recv.at[g]).wait_recv()
             products(g)
 
         @pl.when(k == 2)
@@ -287,48 +282,16 @@
 
     each_peer(lambda peer: dg_copy(peer).start())
 
-    out_h[...] = dot(sel[...], v[...], NT).astype(jnp.bfloat16)
-
-    for q in range(CHUNKS):
-        column_sends(a, q, finish, own=True)
-
-    def drain(k, carry):
-        g = order(k)
-
-        @pl.when(k > 0)
-        def _():
-            for q in range(CHUNKS):
-                column_sends(g, q, finish)
-
-        for j in range(1, nb):
-            for q in range(CHUNKS):
-                cross_sends(g, lax.rem(b + j, nb), q, finish)
-        return carry
-
-    lax.fori_loop(0, ROWS_A, drain, 0)
-
-    def sent(peer):
-        meta_copy(peer).wait_send()
-        slab_copy(peer).wait_send()
-
-    each_peer(sent)
-    grads_over.wait_send()
-    router_over.wait_send()
-
-    own_slab.wait()
-    each_peer(lambda peer: await_from(peer, xs.at[peer], slab_recv.at[peer]))
+    hgv[...] = dot(sel[...], v[...], NT).astype(jnp.bfloat16)
+    hidden_out = pltpu.make_async_copy(hgv, out_h, loc.at[6])
+    hidden_out.start()
     grads_over.wait_recv()
     router_over.wait_recv()
-
-    for j in range(tiles):
-        dg2[j, pl.ds(me, 1), :] = dgo[j : j + 1, :]
-
-    def take(peer):
-        await_from(peer, dgb.at[peer], dg_recv.at[peer])
+    dgb[me] = dgo[...]
+    whole(dgb.at[pl.ds(0, n - 1)], peer_recv.at[1]).wait_recv()
+    for peer in range(n):
         for j in range(tiles):
-            dg2[j, pl.ds(peer, 1), :] = dgb[peer, j : j + 1, :]
-
-    each_peer(take)
+            dg2[j, peer : peer + 1, :] = dgb[peer, j : j + 1, :]
     for j in range(tiles):
         g = jnp.maximum(gt[j], 0.0)
         d = dg2[j]
@@ -336,29 +299,47 @@
     logit_over.start()
 
     lg_all = jnp.concatenate([lg[j] for j in range(tiles)], axis=1)
-    part = dot(lg_all, xs[...].reshape(n * tokens, LANES), NN)
+    part = dot(lg_all, xs[:, :tokens, :].reshape(n * tokens, LANES), NN)
     if feats < LANES:
         shift = lax.rem(LANES - lax.rem(me * feats, LANES), LANES)
         part = pltpu.roll(part, shift, 1)[:, :feats]
-    out_r[...] = part
+    rgv[...] = part
+    router_out = pltpu.make_async_copy(rgv, out_r, loc.at[7])
+    router_out.start()
+
+    for q in range(CHUNKS):
+        column_sends(a, q, finish, own=True)
+
+    def drain(k, carry):
+        g = order(k)
+
+        @pl.when(k > 0)
+        def _():
+            for q in range(CHUNKS):
+                column_sends(g, q, finish)
+
+        if nb > 2:
+            for j in range(1, nb):
+                for q in range(CHUNKS):
+                    cross_sends(g, lax.rem(b + j, nb), q, finish)
+        return carry
+
+    lax.fori_loop(0, ROWS_A, drain, 0)
+    whole(xg.at[pl.ds(0, n // 2)], peer_send.at[2]).wait_send()
+    whole(stage.at[pl.ds(0, n - 1)], peer_send.at[0]).wait_send()
+    whole(dgb.at[pl.ds(0, n - 1)], peer_send.at[1]).wait_send()
+    grads_over.wait_send()
+    router_over.wait_send()
 
     logit_over.wait_recv()
     mine = dot(place, lgn[...], NT).astype(jnp.bfloat16)
-    out_g[...] = (ogn[...].astype(jnp.float32) + dot(mine, rtn[...], NN)).astype(jnp.bfloat16)
-    each_peer(lambda peer: dg_copy(peer).wait_send())
+    outv[...] = (ogn[...].astype(jnp.float32) + dot(mine, rtn[...], NN)).astype(jnp.bfloat16)
+    grads_out = pltpu.make_async_copy(outv, out_g, loc.at[8])
+    grads_out.start()
     logit_over.wait_send()
-
-
-def write_out(grads, hidden, router, out_g, out_h, out_r, sem):
-    copies = [
-        pltpu.make_async_copy(grads, out_g, sem.at[0]),
-        pltpu.make_async_copy(hidden, out_h, sem.at[1]),
-        pltpu.make_async_copy(router, out_r, sem.at[2]),
-    ]
-    for copy in copies:
-        copy.start()
-    for copy in copies:
-        copy.wait()
+    hidden_out.wait()
+    router_out.wait()
+    grads_out.wait()
 
 
 def shards(sections, n, out_grad, layer_input, router_weight, expert_ids, hidden_act, down_weight):
@@ -373,21 +354,20 @@
     bf16, f32 = jnp.bfloat16, jnp.float32
     dma = pltpu.SemaphoreType.DMA
     hbm = pl.BlockSpec(memory_space=pltpu.HBM)
-    vmem = pl.BlockSpec(memory_space=pltpu.VMEM)
     results = (
         jax.ShapeDtypeStruct((tokens, d_model), bf16),
         jax.ShapeDtypeStruct((slots, f_dim), bf16),
         jax.ShapeDtypeStruct((experts, feats), f32),
     )
-    held = pl.pallas_call(
+    grads, hidden, router = pl.pallas_call(
         functools.partial(kernel, sections, n),
         out_shape=results,
         in_specs=[hbm] * 6,
-        out_specs=(vmem,) * 3,
+        out_specs=(hbm,) * 3,
         scratch_shapes=[
             pltpu.VMEM((n, tokens, d_model), bf16),
-            pltpu.VMEM((n, tokens, LANES), bf16),
-            pltpu.VMEM((n, experts, LANES), bf16),
+            pltpu.VMEM((n, tokens + experts, LANES), bf16),
+            pltpu.VMEM((n, tokens + experts, LANES), bf16),
             pltpu.VMEM((n, tiles, LANES), f32),
             pltpu.VMEM((tokens, d_model), bf16),
             pltpu.VMEM((experts, d_model), bf16),
@@ -407,17 +387,17 @@
             pltpu.VMEM((tiles, LANES), f32),
             pltpu.VMEM((tiles, experts, LANES), f32),
             pltpu.VMEM((tiles, experts, LANES), bf16),
+            pltpu.VMEM((tokens, d_model), bf16),
+            pltpu.VMEM((slots, f_dim), bf16),
+            pltpu.VMEM((experts, feats), f32),
             dma((n, CHUNKS)),
             dma((n, CHUNKS, 5)),
-            dma((n,)),
-            dma((n,)),
-            dma((n,)),
-            dma((n,)),
-            dma((n,)),
-            dma((n,)),
+            dma((ROWS_A,)),
+            dma((2,)),
             dma((3,)),
             dma((3,)),
-            dma((7,)),
+            dma((3,)),
+            dma((9,)),
         ],
         compiler_params=pltpu.CompilerParams(
             collective_id=0, has_side_effects=True, vmem_limit_bytes=48 * 2**20
@@ -426,13 +406,6 @@
             flops=2 * total * d_model * f_dim, bytes_accessed=4 * f_dim * d_model, transcendentals=0
         ),
     )(*(pltpu.with_memory_space_constraint(p, pltpu.HBM) for p in (og, x, rt, ids, hid, w)))
-    grads, hidden, router = pl.pallas_call(
-        write_out,
-        out_shape=results,
-        in_specs=[vmem] * 3,
-        out_specs=(hbm,) * 3,
-        scratch_shapes=[dma((3,))],
-    )(*held)
     return (grads[None], hidden[None, None], router.T[None])
 
 

time: 40.9 us -> 38.8 us (0.949)
  Pallas kernels: 38.1 us -> 36.1 us
    pallas_call x1 -> x0, Pallas kernels: 1.78 us -> none  [shards(): pl.pallas_call(write_out, out_shape=results, in_specs=[vmem] * 3, out_spe...]
    unnamed x6 -> x3, local copies, waits for them, and re-layouts: 1.94 us -> 1.97 us
where the time goes in v4:
time: 38.8 us; the launch traced here: 38.7 us
  Pallas kernels  36.1 us (93%)
  local copies, waits for them, and re-layouts  1.97 us (5%)
  between operations  0.64 us (2%)
    pallas_call x1, Pallas kernels, shards(): pl.pallas_call(functools.partial(kernel, sections, n), out_shape=results,...  36.1 us
    unnamed x3, local copies, waits for them, and re-layouts  1.97 us

profile of v4, /device:TPU:0, one launch (start us, length us, event | category | flops | bytes accessed | tf_op | source)
XLA Modules:
  0.0 38.7 jit_solution(487464187394873313)
XLA Ops:
  0.6 36.1 %shard_map.85 = (bf16[32,2048]{1,0:T(8,128)(2,1)S(1)}, bf16[384,384]{1,0:T(8,128)(2,1)S(1)}, f32[16,128]{1,0:T(8,128)S(1)}) custom-call(bf16[32,2048]{1,0:T(8,128)(2,1)} %bitcast.20, bf16[32,2048]{1,0:T(8,128)(2,1)} %bitcast.21, bf16[16,2048]{1,0:T(8,128)(2,1)} %bitcast.22, s32[8,32]{1,0:T(8,128)} %bitcast.23, bf16[384,384]{1,0:T(8,128)(2,1)} %bitcast.19, ...), custom_call_target="tpu_custom_call" | custom-call | flops 805306368 | bytes 3145728 | tf_op jit(solution)/shard_map/pallas_call | solution.py:362
  36.7 0.7 %copy.12 = bf16[1,32,2048]{2,1,0:T(8,128)(2,1)} copy(bf16[1,32,2048]{2,1,0:T(8,128)(2,1)S(1)} %bitcast.16) | data formatting | bytes 262144
  37.4 0.7 %copy.13 = bf16[1,1,384,384]{3,2,1,0:T(8,128)(2,1)} copy(bf16[1,1,384,384]{3,2,1,0:T(8,128)(2,1)S(1)} %bitcast.15) | data formatting | bytes 589824
  38.1 0.6 %copy.14 = f32[1,128,16]{1,2,0:T(8,128)} copy(f32[1,128,16]{1,2,0:T(8,128)S(1)} %bitcast.17) | data formatting | bytes 16384
